TPU v7x, 32 devices: a whole 2x2x4 slice. The times are simulated.
32 devices in a mesh: facet: 2 (over x), vis: 8 (over z, core), spec: 2 (over y).
Axes of the slice: x: 2, y: 2, z: 4, core: 2. Of those that a mesh axis runs over, the one named last changes fastest.
Arguments:
- image: float32 [128, 8, 4096], P(('facet', 'vis'), 'spec'), may hold values from 0 to 1
- wavelet_dual: float32 [128, 8, 4096], P(('facet', 'vis'), 'spec'), may hold values from -6 to 6
- weights: float32 [128, 4096], P(('facet', 'vis')), may hold values from 0.3 to 3
- kernels: bfloat16 [2, 8, 2, 256, 64], P('facet', 'vis'), may hold values from -0.5 to 0.5
- vis_data: bfloat16 [2, 8, 8, 2, 16, 256, 128], P('facet', 'vis', 'spec'), may hold values from -6 to 6
- tile_list: int32 [2, 8, 16], P('facet', 'vis'), may hold values from 0 to 31, as said below
- tile_count: int32 [2, 8], P('facet', 'vis'), may hold values from 4 to 16, as said below
Outputs:
- image_next: float32 [128, 8, 4096], P(('facet', 'vis'), 'spec')
- dual_next: float32 [128, 8, 4096], P(('facet', 'vis'), 'spec')
Inputs may be any that keep to these rules, and one draw needn't show every extreme that they name: `tile_list`: the 16 slots of a block name distinct tiles; slots from tile_count on are unused. `tile_count`: every draw has a block with 16 occupied slots and one with the fewest allowed.
All inputs are finite; a program needn't handle non-finite values.
Results may differ from a plain program's by a relative error of at most 0.017.
Values may be sent and summed in bfloat16 or wider, within the bound.
A program may use at most 128 MiB of HBM per device.

v0:
```python
import functools
import math

import jax
import jax.numpy as jnp
import numpy as np
from jax import lax
from jax.experimental import pallas as pl
from jax.experimental.pallas import tpu as pltpu
from jax.sharding import PartitionSpec as P

MESH = pl.DeviceIdType.MESH
root_three = math.sqrt(3.0)
norm_factor = 4.0 * math.sqrt(2.0)
low_taps = [
    (1.0 + root_three) / norm_factor,
    (3.0 + root_three) / norm_factor,
    (3.0 - root_three) / norm_factor,
    (1.0 - root_three) / norm_factor,
]
high_taps = [low_taps[3], -low_taps[2], low_taps[1], -low_taps[0]]
primal_step = 0.2
dual_step = 0.5
lanes = 128
bf16 = jnp.bfloat16
f32 = jnp.float32


def nn(a, b):
    return jnp.dot(a, b, preferred_element_type=f32)


def nt(a, b):
    return lax.dot_general(a, b, (((1,), (1,)), ((), ())), preferred_element_type=f32)


def tables(rows, chans, width, blocks):
    outer = width // lanes
    half = outer // 2
    tiles = half + 1
    scale = 1.0 / math.sqrt(width)
    one = np.arange(outer)
    small = 2.0 * np.pi * (np.outer(one, one) % outer) / outer
    cos_s, sin_s = np.cos(small), np.sin(small)
    eye_c, eye_r = np.eye(chans), np.eye(rows)
    parts = np.stack([cos_s, -sin_s]) * scale
    fwd_a = np.einsum("pla,cd->cplad", parts, eye_c).reshape(chans * 2 * outer, outer * chans)
    angle = 2.0 * np.pi * (np.outer(np.arange(tiles), np.arange(lanes)) % outer) / outer
    cos_t, sin_t = np.cos(angle), np.sin(angle)
    mix = np.array([[cos_t, sin_t], [-sin_t, cos_t]])
    fwd_b = np.einsum("iptb,rs->tirspb", mix, eye_r).reshape(tiles * 2 * rows, rows * 2 * lanes)
    cos_o, sin_o = cos_t[:, :outer], sin_t[:, :outer]
    mix = np.array([[cos_o, -sin_o], [sin_o, cos_o]])
    inv_t = np.einsum("pitb,rs->rpbtis", mix, eye_r).reshape(rows * 2 * outer, tiles * 2 * rows)
    angle = 2.0 * np.pi * (np.outer(one, np.arange(lanes)) % outer) / outer
    parts = np.stack([np.cos(angle), -np.sin(angle)]) * scale
    inv_l = np.einsum("pal,cd->acdpl", parts, eye_c).reshape(outer * chans, chans * 2 * lanes)
    twist = 2.0 * np.pi * np.outer(np.arange(lanes), np.arange(lanes)) / width
    twist = np.stack([np.cos(twist), np.sin(twist)]).reshape(2, lanes // outer, outer, lanes)
    flip = np.zeros((lanes, lanes))
    for col in range(1, lanes):
        flip[lanes - col, col] = 1.0
    spread = np.zeros((2, blocks, 2, rows, blocks * rows))
    for shard in range(blocks):
        place = (shard % 2) * (blocks // 2) + shard // 2
        for row in range(rows):
            for part in range(2):
                spread[part, place, part, row, shard * rows + row] = 1.0
    spread = spread.reshape(2, blocks * 2 * rows, blocks * rows)
    halves = np.ones((tiles, 2 * rows, lanes))
    halves[0, :, 0] = 0.5
    halves[half, :, 1:] = 0.0
    halves[half, :, 0] = 0.5
    gather_c = np.kron(np.eye(outer), np.ones((1, chans)))

    def b(x):
        return jnp.asarray(x.astype(np.float32), bf16)

    def f(x):
        return jnp.asarray(x.astype(np.float32))

    return [
        b(fwd_a), b(fwd_b), b(inv_t), b(inv_l), f(twist), b(flip), b(spread), f(halves),
        b(gather_c), b(gather_c.T),
    ]


def body(
    total_facets, blocks, rows, chans, slots,
    image_ref, dual_ref, weight_ref, kern_ref, list_ref, count_ref, vis_hbm,
    fwd_a, fwd_b, inv_t, inv_l, twist, flip, spread, halves, gather_c, spread_c,
    next_ref, out_ref,
    grid_ref, full_ref, vis_ref, part_ref, place_ref, back_ref, fold_ref, sib_ref, mine_ref,
    land_ref, ybuf, ubuf, usmall, kfwd, kadj, halo_send, halo_in, ext_ref, ext_send, ext_in,
    upd_ref, own_energy, energy_send, energy_in, pick_s, pos_s, rev_s,
    vis_sem, ag_send, ag_recv, sb_send, sb_recv, fw_send, fw_recv, xs_send, xs_recv,
    rs_send, rs_recv, misc_send, misc_recv,
):
    outer = image_ref.shape[1] // chans
    half = outer // 2
    tiles = half + 1
    nz = blocks // 2
    facet, vis, spec = (lax.axis_index(a) for a in ("facet", "vis", "spec"))
    z = vis // 2
    core = vis % 2
    place = core * nz + z
    position = facet * blocks + vis
    everyone = total_facets * blocks
    after = (position + 1) % everyone
    before = (position + everyone - 1) % everyone
    sibling = {"vis": z * 2 + 1 - core}
    partner = {"spec": 1 - spec}
    next_dev = {"facet": after // blocks, "vis": after % blocks}
    prev_dev = {"facet": before // blocks, "vis": before % blocks}

    def peer(step):
        return {"vis": ((z + step) % nz) * 2 + core}

    vis_copies = [
        pltpu.make_async_copy(vis_hbm.at[c], vis_ref.at[c], vis_sem.at[c]) for c in range(chans)
    ]
    for copy in vis_copies:
        copy.start()

    barrier = pltpu.get_barrier_semaphore()
    greet = [peer(j) for j in range(1, nz)] + [sibling, partner, next_dev, prev_dev]
    for who in greet:
        pl.semaphore_signal(barrier, inc=1, device_id=who, device_id_type=MESH)

    def first(r, _):
        y = nn(fwd_a[...], image_ref[r].astype(bf16))
        cos, sin = twist[0], twist[1]
        for c in range(chans):
            re = y[c * 2 * outer : c * 2 * outer + outer][None]
            im = y[c * 2 * outer + outer : (c + 1) * 2 * outer][None]
            tre = (re * cos + im * sin).reshape(lanes, lanes).astype(bf16)
            tim = (im * cos - re * sin).reshape(lanes, lanes).astype(bf16)
            base = pl.multiple_of(r * 2 * lanes, 2 * lanes)
            ybuf[c, :, pl.ds(base, lanes)] = tre
            ybuf[c, :, pl.ds(pl.multiple_of(base + lanes, lanes), lanes)] = tim
        return 0

    lax.fori_loop(0, rows, first, 0)
    for r in range(3):
        halo_send[r] = dual_ref[rows - 3 + r].astype(bf16)

    def remote(src, dst, send, recv, who):
        return pltpu.make_async_remote_copy(
            src_ref=src, dst_ref=dst, send_sem=send, recv_sem=recv, device_id=who,
            device_id_type=MESH,
        )

    pl.semaphore_wait(barrier, len(greet))
    pending = []
    ag, sb = {}, {}
    for c in range(chans):
        panel = nt(fwd_b[...], ybuf[c]).astype(bf16).reshape(tiles, 2 * rows, lanes)
        grid_ref[c, place] = panel
        for j in range(1, nz):
            ag[c, j] = remote(
                grid_ref.at[c, place], grid_ref.at[c, place],
                ag_send.at[c, j - 1], ag_recv.at[c, j - 1], peer(j),
            )
            ag[c, j].start()
        sb[c] = remote(
            grid_ref.at[c, place], grid_ref.at[c, place], sb_send.at[c], sb_recv.at[c], sibling
        )
        sb[c].start()
    halo = remote(halo_send, halo_in, misc_send.at[0], misc_recv.at[0], next_dev)
    halo.start()

    width_tiles = outer
    for s in range(slots):
        tile = list_ref[s]
        pick_s[s] = jnp.where(tile < half, tile, width_tiles + half - 1 - tile)

    def positions(t, _):
        other = lax.rem(width_tiles - t, width_tiles)
        here, there = jnp.int32(slots), jnp.int32(slots)
        for s in range(slots):
            here = jnp.where(list_ref[s] == t, s, here)
            there = jnp.where(list_ref[s] == other, s, there)
        pos_s[t] = here
        rev_s[t] = there
        return 0

    lax.fori_loop(0, tiles + 1, positions, 0)
    k_re, k_im = kern_ref[0], kern_ref[1]
    top = nn(spread[0], k_re) - nn(spread[1], k_im)
    low = nn(spread[0], k_im) + nn(spread[1], k_re)
    both = jnp.concatenate([top, low], axis=1)
    kadj[...] = both.astype(bf16)
    kfwd[...] = both.T.astype(bf16)
    part_ref[slots] = jnp.zeros(part_ref.shape[1:], bf16)
    count = count_ref[0]

    lane0 = lax.broadcasted_iota(jnp.int32, (1, 2 * rows, lanes), 2) == 0
    sign = jnp.where(
        lax.broadcasted_iota(jnp.int32, (1, 2 * rows, lanes), 1) < rows, 1.0, -1.0
    ).astype(f32)
    tall = blocks * 2 * rows
    meas = vis_ref.shape[3]

    fw, xs, rs = {}, {}, {}

    def scatter(c):
        xs[c].wait_recv()

        def add(s, _):
            theirs = sib_ref[c, s].astype(f32)
            mine_ref[c, s] = (fold_ref[c, core * nz + s].astype(f32) + theirs).astype(bf16)
            return 0

        lax.fori_loop(0, nz, add, 0)
        for j in range(1, nz):
            rs[c, j] = remote(
                mine_ref.at[c, (z + j) % nz], land_ref.at[c, j - 1],
                rs_send.at[c, j - 1], rs_recv.at[c, j - 1], peer(j),
            )
            rs[c, j].start()

    for c in range(chans):
        for j in range(1, nz):
            ag[c, j].wait_recv()
            slot = core * nz + (z + nz - j) % nz
            fw[c, j] = remote(
                grid_ref.at[c, slot], grid_ref.at[c, slot],
                fw_send.at[c, j - 1], fw_recv.at[c, j - 1], sibling,
            )
            fw[c, j].start()
        if c > 0:
            scatter(c - 1)
        sb[c].wait_recv()
        for j in range(1, nz):
            fw[c, j].wait_recv()
        vis_copies[c].wait()

        def unfold(s, _):
            g = grid_ref[c, s]
            full_ref[s, :half] = g[:half]
            back = nn(g[:half].reshape(half * 2 * rows, lanes), flip[...])
            back = back.reshape(half, 2 * rows, lanes)
            back = jnp.where(lane0, g[1:].astype(f32), back) * sign
            full_ref[s, half:] = back.astype(bf16)
            return 0

        lax.fori_loop(0, blocks, unfold, 0)

        def degrid(k, _):
            pair = [2 * k, 2 * k + 1]
            picked = [full_ref[:, pick_s[s]].reshape(tall, lanes) for s in pair]
            pred = nn(kfwd[...], jnp.concatenate(picked, axis=1))
            res = []
            for n, s in enumerate(pair):
                live = (s < count).astype(f32)
                data = vis_ref[c, :, s].reshape(2 * meas, lanes).astype(f32)
                res.append(((pred[:, n * lanes : (n + 1) * lanes] - data) * live).astype(bf16))
            adj = nn(kadj[...], jnp.concatenate(res, axis=1)).astype(bf16)
            for n, s in enumerate(pair):
                part_ref[s] = adj[:, n * lanes : (n + 1) * lanes]
            return 0

        lax.fori_loop(0, slots // 2, degrid, 0)

        def put(t, _):
            place_ref[:, t] = part_ref[pos_s[t]].reshape(blocks, 2 * rows, lanes)
            back_ref[:, t] = part_ref[rev_s[t]].reshape(blocks, 2 * rows, lanes)
            return 0

        lax.fori_loop(0, tiles + 1, put, 0)

        def fold(s, _):
            q = back_ref[s]
            back = nn(q[1:].reshape(tiles * 2 * rows, lanes), flip[...])
            back = back.reshape(tiles, 2 * rows, lanes)
            back = jnp.where(lane0, q[:tiles].astype(f32), back) * sign
            sums = (place_ref[s, :tiles].astype(f32) + back) * halves[...]
            fold_ref[c, s] = sums.astype(bf16)
            return 0

        lax.fori_loop(0, blocks, fold, 0)
        xs[c] = remote(
            fold_ref.at[c, pl.ds((1 - core) * nz, nz)], sib_ref.at[c],
            xs_send.at[c], xs_recv.at[c], sibling,
        )
        xs[c].start()
    scatter(chans - 1)

    for c in range(chans):
        sums = mine_ref[c, z].astype(f32)
        for j in range(1, nz):
            rs[c, j].wait_recv()
            sums = sums + land_ref[c, j - 1].astype(f32)
        flat = sums.astype(bf16).reshape(tiles * 2 * rows, lanes)
        usmall[...] = nn(inv_t[...], flat).reshape(rows, 2, outer, lanes)

        def turn(r, _):
            re, im = usmall[r, 0][None], usmall[r, 1][None]
            cos, sin = twist[0], twist[1]
            tre = (re * cos - im * sin).reshape(lanes, lanes).astype(bf16)
            tim = (re * sin + im * cos).reshape(lanes, lanes).astype(bf16)
            ubuf[r, :, c * 2 * lanes : c * 2 * lanes + lanes] = tre
            ubuf[r, :, c * 2 * lanes + lanes : (c + 1) * 2 * lanes] = tim
            return 0

        lax.fori_loop(0, rows, turn, 0)

    halo.wait_recv()
    has_before = (position > 0).astype(f32)
    has_after = (position < everyone - 1).astype(f32)

    def dual_at(r):
        return dual_ref[r] if r >= 0 else halo_in[r + 3].astype(f32) * has_before

    for r in range(rows):
        grad = nt(inv_l[...], ubuf[r])
        synth = high_taps[0] * dual_at(r)
        for j in range(1, 4):
            synth = synth + high_taps[j] * dual_at(r - j)
        old = image_ref[r]
        new = jnp.maximum(old - primal_step * (grad + synth), 0.0)
        next_ref[r] = new
        ext = 2.0 * new - old
        ext_ref[r] = ext
        if r < 3:
            ext_send[r] = ext.astype(bf16)
        if r == 2:
            rim = remote(ext_send, ext_in, misc_send.at[1], misc_recv.at[1], prev_dev)
            rim.start()

    def ext_at(r):
        return ext_ref[r] if r < rows else ext_in[r - rows].astype(f32) * has_after

    def energies(first_row, last_row, n):
        for r in range(first_row, last_row):
            detail = high_taps[0] * ext_at(r)
            for j in range(1, 4):
                detail = detail + high_taps[j] * ext_at(r + j)
            upd = dual_ref[r] + dual_step * detail
            upd_ref[r] = upd
            square = upd * upd
            hi = square.astype(bf16)
            lo = (square - hi.astype(f32)).astype(bf16)
            energy = nn(gather_c[...], hi) + nn(gather_c[...], lo)
            own_energy[r] = energy
            energy_send[r] = energy.astype(bf16)
        rng = pl.ds(first_row, last_row - first_row)
        copy = remote(
            energy_send.at[rng], energy_in.at[rng], misc_send.at[n], misc_recv.at[n], partner
        )
        copy.start()
        return copy

    def finish(first_row, last_row):
        for r in range(first_row, last_row):
            energy = own_energy[r] + energy_in[r].astype(f32)
            w = weight_ref[:, r, :]
            ratio = w / jnp.maximum(w, jnp.sqrt(energy))
            hi = ratio.astype(bf16)
            lo = (ratio - hi.astype(f32)).astype(bf16)
            out_ref[r] = upd_ref[r] * (nn(spread_c[...], hi) + nn(spread_c[...], lo))

    cut = rows - 3
    early = energies(0, cut, 2)
    rim.wait_recv()
    late = energies(cut, rows, 3)
    early.wait_recv()
    finish(0, cut)
    late.wait_recv()
    finish(cut, rows)

    for copy in [*ag.values(), *sb.values(), *fw.values(), *xs.values(), *rs.values()]:
        copy.wait_send()
    for copy in (halo, rim, early, late):
        copy.wait_send()


def per_device(image, wavelet_dual, weights, kernels, vis_data, tile_list, tile_count):
    rows, chans, width = image.shape
    outer = width // lanes
    facets, blocks = lax.axis_size("facet"), lax.axis_size("vis")
    nz = blocks // 2
    slots = tile_list.shape[-1]
    meas = vis_data.shape[-2]
    tiles = outer // 2 + 1
    tall = blocks * 2 * rows

    def to_rows(x):
        x = x.reshape(rows, chans, outer, lanes).transpose(0, 2, 1, 3)
        return x.reshape(rows, outer * chans, lanes)

    def from_rows(x):
        x = x.reshape(rows, outer, chans, lanes).transpose(0, 2, 1, 3)
        return x.reshape(rows, chans, width)

    consts = tables(rows, chans, width, blocks)
    vmem = pl.BlockSpec(memory_space=pltpu.VMEM)
    smem = pl.BlockSpec(memory_space=pltpu.SMEM)
    sheet = (outer * chans, lanes)
    panel = (tiles, 2 * rows, lanes)
    dma = pltpu.SemaphoreType.DMA
    hop = (chans, nz - 1)
    scratch = [
        pltpu.VMEM((chans, blocks) + panel, bf16),
        pltpu.VMEM((blocks, outer, 2 * rows, lanes), bf16),
        pltpu.VMEM((chans, 2, slots, meas, lanes), bf16),
        pltpu.VMEM((slots + 1, tall, lanes), bf16),
        pltpu.VMEM((blocks, tiles + 1, 2 * rows, lanes), bf16),
        pltpu.VMEM((blocks, tiles + 1, 2 * rows, lanes), bf16),
        pltpu.VMEM((chans, blocks) + panel, bf16),
        pltpu.VMEM((chans, nz) + panel, bf16),
        pltpu.VMEM((chans, nz) + panel, bf16),
        pltpu.VMEM((chans, nz - 1) + panel, bf16),
        pltpu.VMEM((chans, lanes, rows * 2 * lanes), bf16),
        pltpu.VMEM((rows, lanes, chans * 2 * lanes), bf16),
        pltpu.VMEM((rows, 2, outer, lanes), f32),
        pltpu.VMEM((2 * meas, tall), bf16),
        pltpu.VMEM((tall, 2 * meas), bf16),
        pltpu.VMEM((3,) + sheet, bf16),
        pltpu.VMEM((3,) + sheet, bf16),
        pltpu.VMEM((rows,) + sheet, f32),
        pltpu.VMEM((3,) + sheet, bf16),
        pltpu.VMEM((3,) + sheet, bf16),
        pltpu.VMEM((rows,) + sheet, f32),
        pltpu.VMEM((rows, outer, lanes), f32),
        pltpu.VMEM((rows, outer, lanes), bf16),
        pltpu.VMEM((rows, outer, lanes), bf16),
        pltpu.SMEM((slots,), jnp.int32),
        pltpu.SMEM((tiles + 1,), jnp.int32),
        pltpu.SMEM((tiles + 1,), jnp.int32),
        dma((chans,)), dma(hop), dma(hop), dma((chans,)), dma((chans,)), dma(hop), dma(hop),
        dma((chans,)), dma((chans,)), dma(hop), dma(hop), dma((4,)), dma((4,)),
    ]
    shape = jax.ShapeDtypeStruct((rows,) + sheet, f32)
    new, dual = pl.pallas_call(
        functools.partial(body, facets, blocks, rows, chans, slots),
        out_shape=(shape, shape),
        in_specs=[vmem] * 4 + [smem] * 2 + [pl.BlockSpec(memory_space=pl.ANY)]
        + [vmem] * len(consts),
        out_specs=(vmem, vmem),
        scratch_shapes=scratch,
        compiler_params=pltpu.CompilerParams(
            collective_id=0, has_side_effects=True, vmem_limit_bytes=52 * 2**20
        ),
    )(
        to_rows(image),
        to_rows(wavelet_dual),
        weights.reshape(rows, outer, lanes).transpose(1, 0, 2),
        jnp.swapaxes(kernels[0, 0], 1, 2),
        tile_list.reshape(slots),
        tile_count.reshape(1),
        vis_data[0, 0],
        *consts,
    )
    return from_rows(new), from_rows(dual)


def solution(mesh):
    return jax.shard_map(
        per_device,
        mesh=mesh,
        in_specs=(
            P(("facet", "vis"), "spec", None),
            P(("facet", "vis"), "spec", None),
            P(("facet", "vis"), None),
            P("facet", "vis", None, None, None),
            P("facet", "vis", "spec", None, None, None, None),
            P("facet", "vis", None),
            P("facet", "vis"),
        ),
        out_specs=(P(("facet", "vis"), "spec", None), P(("facet", "vis"), "spec", None)),
        check_vma=False,
    )
```

profile of v0, /device:TPU:1, one launch (start us, length us, event | category | flops | bytes accessed | tf_op | source)
XLA Modules:
  0.0 80.0 jit_solution(1771016628822300591)
XLA Ops:
  1.3 0.0 copy-start
  1.3 1.0 %copy-done = bf16[512,272]{1,0:T(8,128)(2,1)S(1)} copy-done((bf16[512,272]{1,0:T(8,128)(2,1)S(1)}, bf16[512,272]{1,0:T(8,128)(2,1)}, u32[]{:S(2)}) %copy-start) | copy-done | bytes 278552
  2.3 0.0 copy-start.1
  2.3 0.9 %copy-done.1 = bf16[128,1024]{1,0:T(8,128)(2,1)S(1)} copy-done((bf16[128,1024]{1,0:T(8,128)(2,1)S(1)}, bf16[128,1024]{1,0:T(8,128)(2,1)}, u32[]{:S(2)}) %copy-start.1) | copy-done | bytes 262168
  3.2 0.0 copy-start.2
  3.2 0.9 %copy-done.2 = f32[17,16,128]{2,1,0:T(8,128)S(1)} copy-done((f32[17,16,128]{2,1,0:T(8,128)S(1)}, f32[17,16,128]{2,1,0:T(8,128)}, u32[]{:S(2)}) %copy-start.2) | copy-done | bytes 139288
  4.1 0.0 copy-start.3
  4.1 0.9 %copy-done.3 = f32[8,4096]{1,0:T(8,128)S(1)} copy-done((f32[8,4096]{1,0:T(8,128)S(1)}, f32[8,4096]{1,0:T(8,128)}, u32[]{:S(2)}) %copy-start.3) | copy-done | bytes 131096
  5.0 0.0 copy-start.4
  5.0 0.9 %copy-done.4 = f32[2,4,32,128]{3,2,1,0:T(8,128)S(1)} copy-done((f32[2,4,32,128]{3,2,1,0:T(8,128)S(1)}, f32[2,4,32,128]{3,2,1,0:T(8,128)}, u32[]{:S(2)}) %copy-start.4) | copy-done | bytes 131096
  5.9 0.0 copy-start.5
  5.9 0.8 %copy-done.5 = bf16[1,1,2,256,64]{3,4,2,1,0:T(8,128)(2,1)S(1)} copy-done((bf16[1,1,2,256,64]{3,4,2,1,0:T(8,128)(2,1)S(1)}, bf16[1,1,2,256,64]{3,4,2,1,0:T(8,128)(2,1)}, u32[]{:S(2)}) %copy-start.5) | copy-done | bytes 65560
  6.8 0.0 copy-start.6
  6.8 0.8 %copy-done.6 = bf16[2,128,64]{2,1,0:T(8,128)(2,1)S(1)} copy-done((bf16[2,128,64]{2,1,0:T(8,128)(2,1)S(1)}, bf16[2,128,64]{2,1,0:T(8,128)(2,1)}, u32[]{:S(2)}) %copy-start.6) | copy-done | bytes 32792
  7.6 0.0 copy-start.7
  7.6 0.8 %copy-done.7 = bf16[256,128]{1,0:T(8,128)(2,1)S(1)} copy-done((bf16[256,128]{1,0:T(8,128)(2,1)S(1)}, bf16[256,128]{1,0:T(8,128)(2,1)}, u32[]{:S(2)}) %copy-start.7) | copy-done | bytes 65560
  8.5 0.0 copy-start.8
  8.5 0.8 copy-done.8
  9.2 0.0 copy-start.9
  9.2 0.8 copy-done.9
  10.0 0.0 copy-start.10
  10.0 0.7 copy-done.10
  10.7 0.0 copy-start.11
  10.7 0.7 copy-done.11
  11.3 66.0 %shard_map.176 = (f32[8,128,128]{2,1,0:T(8,128)S(1)}, f32[8,128,128]{2,1,0:T(8,128)}) custom-call(f32[8,128,128]{2,1,0:T(8,128)} %bitcast.35, f32[8,128,128]{2,1,0:T(8,128)} %bitcast.36, f32[32,8,128]{2,1,0:T(8,128)S(1)} %bitcast.31, bf16[2,64,256]{2,1,0:T(8,128)(2,1)S(1)} %bitcast.32, s32[16]{0:T(128)S(1)} %bitcast.33, s32[1]{0:T(128)} %bitcast.29.count_ref, ...), custom_call_target="tpu_custom_call" | custom-call | tf_op jit(solution)/shard_map/pallas_call | solution.py:435
  77.3 0.8 copy.26
  78.1 1.9 %copy.27 = f32[8,4,4096]{2,1,0:T(4,128)} copy(f32[8,4,4096]{2,1,0:T(4,128)} %bitcast.37) | data formatting | bytes 1048576
Async XLA Ops:
  1.3 1.0 %copy-start = (bf16[512,272]{1,0:T(8,128)(2,1)S(1)}, bf16[512,272]{1,0:T(8,128)(2,1)}, u32[]{:S(2)}) copy-start(bf16[512,272]{1,0:T(8,128)(2,1)} %constant.22.clone.inv_t) | copy-start | bytes 835588
  2.3 0.9 %copy-start.1 = (bf16[128,1024]{1,0:T(8,128)(2,1)S(1)}, bf16[128,1024]{1,0:T(8,128)(2,1)}, u32[]{:S(2)}) copy-start(bf16[128,1024]{1,0:T(8,128)(2,1)} %constant.23.clone.inv_l) | copy-start | bytes 786436
  3.2 0.9 %copy-start.2 = (f32[17,16,128]{2,1,0:T(8,128)S(1)}, f32[17,16,128]{2,1,0:T(8,128)}, u32[]{:S(2)}) copy-start(f32[17,16,128]{2,1,0:T(8,128)} %constant.27.clone.halves) | copy-start | bytes 417796
  4.1 0.9 %copy-start.3 = (f32[8,4096]{1,0:T(8,128)S(1)}, f32[8,4096]{1,0:T(8,128)}, u32[]{:S(2)}) copy-start(f32[8,4096]{1,0:T(8,128)} %param.19) | copy-start | bytes 393220
  5.0 0.9 %copy-start.4 = (f32[2,4,32,128]{3,2,1,0:T(8,128)S(1)}, f32[2,4,32,128]{3,2,1,0:T(8,128)}, u32[]{:S(2)}) copy-start(f32[2,4,32,128]{3,2,1,0:T(8,128)} %constant.24.clone.twist) | copy-start | bytes 393220
  5.9 0.8 %copy-start.5 = (bf16[1,1,2,256,64]{3,4,2,1,0:T(8,128)(2,1)S(1)}, bf16[1,1,2,256,64]{3,4,2,1,0:T(8,128)(2,1)}, u32[]{:S(2)}) copy-start(bf16[1,1,2,256,64]{3,4,2,1,0:T(8,128)(2,1)} %param.20) | copy-start | bytes 196612
  6.8 0.8 %copy-start.6 = (bf16[2,128,64]{2,1,0:T(8,128)(2,1)S(1)}, bf16[2,128,64]{2,1,0:T(8,128)(2,1)}, u32[]{:S(2)}) copy-start(bf16[2,128,64]{2,1,0:T(8,128)(2,1)} %constant.26.clone.spread) | copy-start | bytes 98308
  7.6 0.8 %copy-start.7 = (bf16[256,128]{1,0:T(8,128)(2,1)S(1)}, bf16[256,128]{1,0:T(8,128)(2,1)}, u32[]{:S(2)}) copy-start(bf16[256,128]{1,0:T(8,128)(2,1)} %constant.20.clone.fwd_a) | copy-start | bytes 196612
  8.5 0.8 copy-start.8
  9.2 0.8 copy-start.9
  10.0 0.7 copy-start.10
  10.7 0.7 copy-start.11
where the time goes:
time: 80.8 us; the launch traced here: 80 us
  Pallas kernels  66 us (82%)
  local copies, waits for them, and re-layouts  12.7 us (16%)
  between operations  1.31 us (2%)
    pallas_call x1, Pallas kernels, per_device(): pl.pallas_call(functools.partial(body, facets, blocks, rows, chans, slots...  66 us
    unnamed x26, local copies, waits for them, and re-layouts  12.7 us

commit v1 on v0

--- a/solution.py
+++ b/solution.py
@@ -86,16 +86,26 @@
 
 
 def body(
-    total_facets, blocks, rows, chans, slots,
-    image_ref, dual_ref, weight_ref, kern_ref, list_ref, count_ref, vis_hbm,
-    fwd_a, fwd_b, inv_t, inv_l, twist, flip, spread, halves, gather_c, spread_c,
-    next_ref, out_ref,
+    loads, total_facets, blocks, rows, chans, slots,
+    *refs,
+):
+    names = len(loads) + 1
+    sources, vis_hbm = refs[: names - 1], refs[names - 1]
+    next_ref, out_ref = refs[names : names + 2]
+    held = refs[names + 2 : 2 * names + 1]
+    (
+        image_ref, dual_ref, weight_ref, kern_ref, list_ref, count_ref,
+        fwd_a, fwd_b, inv_t, inv_l, twist, flip, spread, halves, gather_c, spread_c,
+    ) = held
+    load_sem = refs[2 * names + 1]
+    (
     grid_ref, full_ref, vis_ref, part_ref, place_ref, back_ref, fold_ref, sib_ref, mine_ref,
     land_ref, ybuf, ubuf, usmall, kfwd, kadj, halo_send, halo_in, ext_ref, ext_send, ext_in,
     upd_ref, own_energy, energy_send, energy_in, pick_s, pos_s, rev_s,
     vis_sem, ag_send, ag_recv, sb_send, sb_recv, fw_send, fw_recv, xs_send, xs_recv,
-    rs_send, rs_recv, misc_send, misc_recv,
-):
+    rs_send, rs_recv, misc_send, misc_recv, sum_ref, relay_ref,
+    rl_send, relay_send, relay_recv,
+    ) = refs[2 * names + 2 :]
     outer = image_ref.shape[1] // chans
     half = outer // 2
     tiles = half + 1
@@ -113,19 +123,42 @@
     next_dev = {"facet": after // blocks, "vis": after % blocks}
     prev_dev = {"facet": before // blocks, "vis": before % blocks}
 
+    def to(step):
+        if nz == 4:
+            return [z + 1 - 2 * (z % 2), (z + 2) % 4, 3 - z][step - 1]
+        return (z + step) % nz
+
+    def source(step):
+        return to(step) if nz == 4 else (z + nz - step) % nz
+
     def peer(step):
-        return {"vis": ((z + step) % nz) * 2 + core}
-
+        return {"vis": to(step) * 2 + core}
+
+    short = nz == 4
+    inner = z % 3 != 0
+
+    loading = [
+        pltpu.make_async_copy(src, dst, load_sem.at[n])
+        for n, (src, dst) in enumerate(zip(sources, held))
+    ]
+    head, middle, last = [0, 6, 10, 7, 1], [3, 12, 4, 5, 11, 13], [8, 9, 2, 14, 15]
+    for n in head + middle:
+        loading[n].start()
     vis_copies = [
         pltpu.make_async_copy(vis_hbm.at[c], vis_ref.at[c], vis_sem.at[c]) for c in range(chans)
     ]
     for copy in vis_copies:
         copy.start()
+    for n in last:
+        loading[n].start()
 
     barrier = pltpu.get_barrier_semaphore()
     greet = [peer(j) for j in range(1, nz)] + [sibling, partner, next_dev, prev_dev]
     for who in greet:
         pl.semaphore_signal(barrier, inc=1, device_id=who, device_id_type=MESH)
+
+    for n in head:
+        loading[n].wait()
 
     def first(r, _):
         y = nn(fwd_a[...], image_ref[r].astype(bf16))
@@ -161,7 +194,10 @@
                 grid_ref.at[c, place], grid_ref.at[c, place],
                 ag_send.at[c, j - 1], ag_recv.at[c, j - 1], peer(j),
             )
-            ag[c, j].start()
+            if short and j == 3:
+                pl.when(inner)(ag[c, j].start)
+            else:
+                ag[c, j].start()
         sb[c] = remote(
             grid_ref.at[c, place], grid_ref.at[c, place], sb_send.at[c], sb_recv.at[c], sibling
         )
@@ -170,6 +206,8 @@
     halo.start()
 
     width_tiles = outer
+    for n in middle:
+        loading[n].wait()
     for s in range(slots):
         tile = list_ref[s]
         pick_s[s] = jnp.where(tile < half, tile, width_tiles + half - 1 - tile)
@@ -201,7 +239,19 @@
     tall = blocks * 2 * rows
     meas = vis_ref.shape[3]
 
-    fw, xs, rs = {}, {}, {}
+    fw, xs, rs, extra, relayed = {}, {}, {}, {}, {}
+
+    def relay(c):
+        if not short:
+            return
+
+        @pl.when(inner)
+        def _():
+            extra[c].wait_recv()
+            there = to(2)
+            both = mine_ref[c, there].astype(f32) + relay_ref[c].astype(f32)
+            mine_ref[c, there] = both.astype(bf16)
+            rs[c, 2].start()
 
     def scatter(c):
         xs[c].wait_recv()
@@ -214,22 +264,42 @@
         lax.fori_loop(0, nz, add, 0)
         for j in range(1, nz):
             rs[c, j] = remote(
-                mine_ref.at[c, (z + j) % nz], land_ref.at[c, j - 1],
+                mine_ref.at[c, to(j)], land_ref.at[c, j - 1],
                 rs_send.at[c, j - 1], rs_recv.at[c, j - 1], peer(j),
             )
-            rs[c, j].start()
-
-    for c in range(chans):
-        for j in range(1, nz):
+            if not short:
+                rs[c, j].start()
+        if short:
+            extra[c] = remote(
+                mine_ref.at[c, to(3)], relay_ref.at[c], relay_send.at[c], relay_recv.at[c], peer(1)
+            )
+            pl.when(jnp.logical_not(inner))(extra[c].start)
+            rs[c, 1].start()
+            pl.when(jnp.logical_not(inner))(rs[c, 2].start)
+            pl.when(inner)(rs[c, 3].start)
+
+    def pass_on(c, steps):
+        for j in steps:
             ag[c, j].wait_recv()
-            slot = core * nz + (z + nz - j) % nz
+            slot = core * nz + source(j)
+            if short and j == 2:
+                relayed[c] = remote(
+                    grid_ref.at[c, slot], grid_ref.at[c, slot],
+                    rl_send.at[c], ag_recv.at[c, 2], peer(1),
+                )
+                pl.when(inner)(relayed[c].start)
             fw[c, j] = remote(
                 grid_ref.at[c, slot], grid_ref.at[c, slot],
                 fw_send.at[c, j - 1], fw_recv.at[c, j - 1], sibling,
             )
             fw[c, j].start()
+
+    for c in range(chans):
+        pass_on(c, (2, 1) if short else range(1, nz))
         if c > 0:
             scatter(c - 1)
+        if short:
+            pass_on(c, (3,))
         sb[c].wait_recv()
         for j in range(1, nz):
             fw[c, j].wait_recv()
@@ -284,14 +354,27 @@
             xs_send.at[c], xs_recv.at[c], sibling,
         )
         xs[c].start()
+        if c > 0:
+            relay(c - 1)
     scatter(chans - 1)
+    relay(chans - 1)
+    for n in last:
+        loading[n].wait()
 
     for c in range(chans):
         sums = mine_ref[c, z].astype(f32)
-        for j in range(1, nz):
+        for j in range(1, 3 if short else nz):
             rs[c, j].wait_recv()
             sums = sums + land_ref[c, j - 1].astype(f32)
-        flat = sums.astype(bf16).reshape(tiles * 2 * rows, lanes)
+        sum_ref[...] = sums
+        if short:
+
+            @pl.when(inner)
+            def _():
+                rs[c, 3].wait_recv()
+                sum_ref[...] += land_ref[c, 2].astype(f32)
+
+        flat = sum_ref[...].astype(bf16).reshape(tiles * 2 * rows, lanes)
         usmall[...] = nn(inv_t[...], flat).reshape(rows, 2, outer, lanes)
 
         def turn(r, _):
@@ -369,8 +452,27 @@
     late.wait_recv()
     finish(cut, rows)
 
-    for copy in [*ag.values(), *sb.values(), *fw.values(), *xs.values(), *rs.values()]:
+    some = []
+    for copies in (ag, rs):
+        for (c, j), copy in copies.items():
+            if short and j == 3:
+                some.append(copy)
+            else:
+                copy.wait_send()
+    for copy in [*sb.values(), *fw.values(), *xs.values()]:
         copy.wait_send()
+    if short:
+
+        @pl.when(inner)
+        def _():
+            for copy in [*some, *relayed.values()]:
+                copy.wait_send()
+
+        @pl.when(jnp.logical_not(inner))
+        def _():
+            for copy in extra.values():
+                copy.wait_send()
+
     for copy in (halo, rim, early, late):
         copy.wait_send()
 
@@ -395,7 +497,6 @@
 
     consts = tables(rows, chans, width, blocks)
     vmem = pl.BlockSpec(memory_space=pltpu.VMEM)
-    smem = pl.BlockSpec(memory_space=pltpu.SMEM)
     sheet = (outer * chans, lanes)
     panel = (tiles, 2 * rows, lanes)
     dma = pltpu.SemaphoreType.DMA
@@ -430,28 +531,34 @@
         pltpu.SMEM((tiles + 1,), jnp.int32),
         dma((chans,)), dma(hop), dma(hop), dma((chans,)), dma((chans,)), dma(hop), dma(hop),
         dma((chans,)), dma((chans,)), dma(hop), dma(hop), dma((4,)), dma((4,)),
+        pltpu.VMEM(panel, f32),
+        pltpu.VMEM((chans,) + panel, bf16),
+        dma((chans,)), dma((chans,)), dma((chans,)),
     ]
-    shape = jax.ShapeDtypeStruct((rows,) + sheet, f32)
-    new, dual = pl.pallas_call(
-        functools.partial(body, facets, blocks, rows, chans, slots),
-        out_shape=(shape, shape),
-        in_specs=[vmem] * 4 + [smem] * 2 + [pl.BlockSpec(memory_space=pl.ANY)]
-        + [vmem] * len(consts),
-        out_specs=(vmem, vmem),
-        scratch_shapes=scratch,
-        compiler_params=pltpu.CompilerParams(
-            collective_id=0, has_side_effects=True, vmem_limit_bytes=52 * 2**20
-        ),
-    )(
+    operands = [
         to_rows(image),
         to_rows(wavelet_dual),
         weights.reshape(rows, outer, lanes).transpose(1, 0, 2),
         jnp.swapaxes(kernels[0, 0], 1, 2),
         tile_list.reshape(slots),
         tile_count.reshape(1),
-        vis_data[0, 0],
         *consts,
-    )
+    ]
+    held = [
+        (pltpu.SMEM if x.dtype == jnp.int32 else pltpu.VMEM)(x.shape, x.dtype) for x in operands
+    ]
+    scratch = [*held, dma((len(operands),)), *scratch]
+    shape = jax.ShapeDtypeStruct((rows,) + sheet, f32)
+    new, dual = pl.pallas_call(
+        functools.partial(body, operands, facets, blocks, rows, chans, slots),
+        out_shape=(shape, shape),
+        in_specs=[pl.BlockSpec(memory_space=pltpu.HBM)] * (len(operands) + 1),
+        out_specs=(vmem, vmem),
+        scratch_shapes=scratch,
+        compiler_params=pltpu.CompilerParams(
+            collective_id=0, has_side_effects=True, vmem_limit_bytes=64 * 2**20
+        ),
+    )(*operands, vis_data[0, 0])
     return from_rows(new), from_rows(dual)
 
 

time: 80.8 us -> 77.1 us (0.954)
  local copies, waits for them, and re-layouts: 12.7 us -> 3.74 us
  Pallas kernels: 66 us -> 71.2 us
    unnamed x26 -> x2, local copies, waits for them, and re-layouts: 12.7 us -> 3.74 us
    pallas_call x1, Pallas kernels: 66 us -> 71.2 us  [per_device(): pl.pallas_call(functools.partial(body, operands, facets, blocks, rows, ch...]
where the time goes in v1:
time: 77.1 us; the launch traced here: 76.2 us
  Pallas kernels  71.2 us (92%)
  local copies, waits for them, and re-layouts  3.74 us (5%)
  between operations  1.29 us (2%)
    pallas_call x1, Pallas kernels, per_device(): pl.pallas_call(functools.partial(body, operands, facets, blocks, rows, ch...  71.2 us
    unnamed x2, local copies, waits for them, and re-layouts  3.74 us

profile of v1, /device:TPU:1, one launch (start us, length us, event | category | flops | bytes accessed | tf_op | source)
XLA Modules:
  0.0 76.2 jit_solution(17383994965237525483)
XLA Ops:
  1.3 71.2 %shard_map.176 = (f32[8,128,128]{2,1,0:T(8,128)}, f32[8,128,128]{2,1,0:T(8,128)}) custom-call(f32[8,128,128]{2,1,0:T(8,128)} %bitcast.31, f32[8,128,128]{2,1,0:T(8,128)} %bitcast.32, f32[32,8,128]{2,1,0:T(8,128)} %bitcast.35, bf16[2,64,256]{2,1,0:T(8,128)(2,1)} %bitcast.36, s32[16]{0:T(128)} %bitcast.37, s32[1]{0:T(128)} %bitcast.29.refs_5_, ...), custom_call_target="tpu_custom_call" | custom-call | tf_op jit(solution)/shard_map/pallas_call | solution.py:552
  72.5 1.9 %copy.26 = f32[8,4,4096]{2,1,0:T(4,128)} copy(f32[8,4,4096]{2,1,0:T(4,128)} %bitcast.34) | data formatting | bytes 1048576
  74.4 1.9 %copy.27 = f32[8,4,4096]{2,1,0:T(4,128)} copy(f32[8,4,4096]{2,1,0:T(4,128)} %bitcast.33) | data formatting | bytes 1048576

commit v2 on v1

--- a/solution.py
+++ b/solution.py
@@ -134,7 +134,8 @@
     def peer(step):
         return {"vis": to(step) * 2 + core}
 
-    short = nz == 4
+    short = False
+    ahead = min(4, chans)
     inner = z % 3 != 0
 
     loading = [
@@ -186,9 +187,21 @@
     pl.semaphore_wait(barrier, len(greet))
     pending = []
     ag, sb = {}, {}
-    for c in range(chans):
-        panel = nt(fwd_b[...], ybuf[c]).astype(bf16).reshape(tiles, 2 * rows, lanes)
-        grid_ref[c, place] = panel
+    first_lane = lax.broadcasted_iota(jnp.int32, (rows, lanes), 1) == 0
+
+    def pack(panel):
+        im = jnp.where(first_lane, panel[half, :rows], panel[0, rows:])
+        return jnp.concatenate([jnp.concatenate([panel[0, :rows], im], 0)[None], panel[1:half]], 0)
+
+    def unpack(panel):
+        im = panel[0, rows:]
+        low = jnp.concatenate([panel[0, :rows], jnp.where(first_lane, 0.0, im)], 0)
+        middle = jnp.concatenate([jnp.where(first_lane, im, 0.0), jnp.zeros_like(im)], 0)
+        return jnp.concatenate([low[None], panel[1:], middle[None]], 0)
+
+    def send_panel(c):
+        panel = nt(fwd_b[...], ybuf[c]).reshape(tiles, 2 * rows, lanes)
+        grid_ref[c, place] = pack(panel).astype(bf16)
         for j in range(1, nz):
             ag[c, j] = remote(
                 grid_ref.at[c, place], grid_ref.at[c, place],
@@ -202,6 +215,9 @@
             grid_ref.at[c, place], grid_ref.at[c, place], sb_send.at[c], sb_recv.at[c], sibling
         )
         sb[c].start()
+
+    for c in range(ahead):
+        send_panel(c)
     halo = remote(halo_send, halo_in, misc_send.at[0], misc_recv.at[0], next_dev)
     halo.start()
 
@@ -296,6 +312,8 @@
 
     for c in range(chans):
         pass_on(c, (2, 1) if short else range(1, nz))
+        if c + ahead < chans:
+            send_panel(c + ahead)
         if c > 0:
             scatter(c - 1)
         if short:
@@ -306,11 +324,12 @@
         vis_copies[c].wait()
 
         def unfold(s, _):
-            g = grid_ref[c, s]
-            full_ref[s, :half] = g[:half]
-            back = nn(g[:half].reshape(half * 2 * rows, lanes), flip[...])
+            g = unpack(grid_ref[c, s].astype(f32))
+            low = g[:half].astype(bf16)
+            full_ref[s, :half] = low
+            back = nn(low.reshape(half * 2 * rows, lanes), flip[...])
             back = back.reshape(half, 2 * rows, lanes)
-            back = jnp.where(lane0, g[1:].astype(f32), back) * sign
+            back = jnp.where(lane0, g[1:], back) * sign
             full_ref[s, half:] = back.astype(bf16)
             return 0
 
@@ -345,7 +364,7 @@
             back = back.reshape(tiles, 2 * rows, lanes)
             back = jnp.where(lane0, q[:tiles].astype(f32), back) * sign
             sums = (place_ref[s, :tiles].astype(f32) + back) * halves[...]
-            fold_ref[c, s] = sums.astype(bf16)
+            fold_ref[c, s] = pack(sums).astype(bf16)
             return 0
 
         lax.fori_loop(0, blocks, fold, 0)
@@ -374,7 +393,7 @@
                 rs[c, 3].wait_recv()
                 sum_ref[...] += land_ref[c, 2].astype(f32)
 
-        flat = sum_ref[...].astype(bf16).reshape(tiles * 2 * rows, lanes)
+        flat = unpack(sum_ref[...]).astype(bf16).reshape(tiles * 2 * rows, lanes)
         usmall[...] = nn(inv_t[...], flat).reshape(rows, 2, outer, lanes)
 
         def turn(r, _):
@@ -498,7 +517,7 @@
     consts = tables(rows, chans, width, blocks)
     vmem = pl.BlockSpec(memory_space=pltpu.VMEM)
     sheet = (outer * chans, lanes)
-    panel = (tiles, 2 * rows, lanes)
+    panel = (outer // 2, 2 * rows, lanes)
     dma = pltpu.SemaphoreType.DMA
     hop = (chans, nz - 1)
     scratch = [

time: 77.1 us -> 69.8 us (0.905)
  Pallas kernels: 71.2 us -> 64.6 us
    pallas_call x1, Pallas kernels: 71.2 us -> 64.6 us  [per_device(): pl.pallas_call(functools.partial(body, operands, facets, blocks, rows, ch...]
where the time goes in v2:
time: 69.8 us; the launch traced here: 69.6 us
  Pallas kernels  64.6 us (93%)
  local copies, waits for them, and re-layouts  3.74 us (5%)
  between operations  1.29 us (2%)
    pallas_call x1, Pallas kernels, per_device(): pl.pallas_call(functools.partial(body, operands, facets, blocks, rows, ch...  64.6 us
    unnamed x2, local copies, waits for them, and re-layouts  3.74 us

profile of v2, /device:TPU:1, one launch (start us, length us, event | category | flops | bytes accessed | tf_op | source)
XLA Modules:
  0.0 69.6 jit_solution(7557218676610480444)
XLA Ops:
  1.3 64.6 %shard_map.176 = (f32[8,128,128]{2,1,0:T(8,128)}, f32[8,128,128]{2,1,0:T(8,128)}) custom-call(f32[8,128,128]{2,1,0:T(8,128)} %bitcast.31, f32[8,128,128]{2,1,0:T(8,128)} %bitcast.32, f32[32,8,128]{2,1,0:T(8,128)} %bitcast.35, bf16[2,64,256]{2,1,0:T(8,128)(2,1)} %bitcast.36, s32[16]{0:T(128)} %bitcast.37, s32[1]{0:T(128)} %bitcast.29.refs_5_, ...), custom_call_target="tpu_custom_call" | custom-call | tf_op jit(solution)/shard_map/pallas_call | solution.py:571
  65.9 1.9 %copy.26 = f32[8,4,4096]{2,1,0:T(4,128)} copy(f32[8,4,4096]{2,1,0:T(4,128)} %bitcast.34) | data formatting | bytes 1048576
  67.7 1.9 %copy.27 = f32[8,4,4096]{2,1,0:T(4,128)} copy(f32[8,4,4096]{2,1,0:T(4,128)} %bitcast.33) | data formatting | bytes 1048576
